TPU v7x, 128 devices: a whole 4x4x4 slice. The times are simulated.
128 devices in a mesh: grp: 4 (over x), seq: 16 (over z, y), head: 2 (over core).
Axes of the slice: x: 4, y: 4, z: 4, core: 2. Of those that a mesh axis runs over, the one named last changes fastest.
Arguments:
- enc_ids: int32 [32, 1024], P('grp', 'seq'), may hold values from 0 to 32127
- lengths: int32 [32], P('grp'), may hold values from 1 to 924, as said below
- dec_ids: int32 [32, 128], P('grp', 'seq'), may hold values from 0 to 32127
- target_ids: int32 [32, 128], P('grp', 'seq'), may hold values from 0 to 32127
- loss_mask: int32 [32, 128], P('grp'), may hold values from 0 to 1, as said below
- embedding: bfloat16 [32128, 768], P('head')
- prompt: float32 [100, 768], replicated, may hold values from -6 to 6
- first_moment: float32 [100, 768], replicated, may hold values from -5.722046e-06 to 5.722046e-06
- second_moment: float32 [100, 768], replicated, may hold values from 1.3020833e-13 to 5.208333e-13
- gains: float32 [7, 768], replicated, may hold values from 0.5 to 1.5
- enc_qkv: bfloat16 [768, 2304], replicated, may hold values from -0.21875 to 0.21875
- enc_wo: bfloat16 [768, 768], replicated, may hold values from -0.875 to 0.875
- enc_w1: bfloat16 [768, 3072], replicated, may hold values from -0.21875 to 0.21875
- enc_w2: bfloat16 [3072, 768], replicated, may hold values from -0.109375 to 0.109375
- dec_qkv: bfloat16 [768, 3, 768], P(None, None, 'head'), may hold values from -0.21875 to 0.21875
- dec_wo: bfloat16 [768, 768], P('head'), may hold values from -0.625 to 0.625
- cross_q: bfloat16 [768, 768], P(None, 'head'), may hold values from -0.21875 to 0.21875
- cross_kv: bfloat16 [768, 2, 768], P(None, None, 'head'), may hold values from -0.21875 to 0.21875
- cross_wo: bfloat16 [768, 768], P('head'), may hold values from -0.875 to 0.875
- dec_w1: bfloat16 [768, 3072], P(None, 'head'), may hold values from -0.21875 to 0.21875
- dec_w2: bfloat16 [3072, 768], P('head'), may hold values from -0.109375 to 0.109375
Outputs:
- loss: float32 [], replicated
- grad_norm: float32 [], replicated
- trust_norms: float32 [2], replicated
- first_new: float32 [100, 768], replicated
- second_new: float32 [100, 768], replicated
- prompt_new: float32 [100, 768], replicated
Inputs may be any that keep to these rules, and one draw needn't show every extreme that they name: `lengths`: in each group of 8 consecutive examples one has exactly 924 input tokens. `loss_mask`: the first target of every example counts.
All inputs are finite; a program needn't handle non-finite values.
Results may differ from a plain program's by a relative error of at most 0.00355.
Values may be sent and summed in bfloat16 or wider, within the bound.
A program may use at most 256 MiB of HBM per device.

v0:
```python
import jax
import jax.numpy as jnp
from jax import lax
from jax.experimental import pallas as pl
from jax.experimental.pallas import tpu as pltpu
from jax.sharding import Mesh
from jax.sharding import PartitionSpec as P

HD = 64
PROMPT = 100
STEP = 5
QUARTERS = 4
SEQ = ("ex", "chip")
CLUSTER = ("chip", "head")
EVERYONE = ("grp", "ex", "chip", "head")
NEG = -1000000000.0

norm_eps = 1e-06
beta_first = 0.5
beta_second = 0.5
adam_eps = 1e-12
decay_rate = 0.01
learn_rate = 0.3
clip_bound = 0.0001


MESH = pl.DeviceIdType.MESH
BF = jnp.bfloat16
F32 = jnp.float32
LEAD_PAD = 32
CHUNK = 1024
RING = 4
LANES = 128


def dot_nn(left, right):
    return lax.dot_general(left, right, (((1,), (0,)), ((), ())), preferred_element_type=F32)


def dot_nt(left, right):
    return lax.dot_general(left, right, (((1,), (1,)), ((), ())), preferred_element_type=F32)


def dot_tn(left, right):
    return lax.dot_general(left, right, (((0,), (0,)), ((), ())), preferred_element_type=F32)


def rms(value, gain):
    return value * lax.rsqrt(jnp.mean(value * value, axis=-1, keepdims=True) + norm_eps) * gain


def rms_grad(value, gain, grad):
    scale = lax.rsqrt(jnp.mean(value * value, axis=-1, keepdims=True) + norm_eps)
    scaled = grad * gain
    inner = jnp.mean(scaled * value, axis=-1, keepdims=True)
    return scale * scaled - value * (scale * scale * scale * inner)


GELU_A = 0.7978845608028654
GELU_B = 0.044715


def gelu(value):
    return 0.5 * value * (1.0 + jnp.tanh(GELU_A * (value + GELU_B * (value * value * value))))


def gelu_grad(value, grad):
    square = value * value
    bend = jnp.tanh(GELU_A * (value + GELU_B * (square * value)))
    slope = 0.5 * (1.0 + bend) + 0.5 * value * (1.0 - bend * bend) * (GELU_A * (1.0 + 3.0 * GELU_B * square))
    return grad * slope


def tiles(count, size, body):
    def step(index, carry):
        body(pl.ds(pl.multiple_of(index * size, size), size))
        return carry

    lax.fori_loop(0, count, step, 0)


def main_kernel(
    picked, lead, ok_all, ok_chip, ok_lead, weight, gains,
    enc_qkv, enc_wo, enc_w1, enc_w2, dec_qkv, dec_wo, cross_q, cross_kv, cross_wo, dec_w1, dec_w2, embedding,
    out,
    w_qkv, w_o, w_1, w_2, w_dqkv, w_do, w_cq, w_ckv, w_co, w_d1, w_d2, ring,
    enc_my, enc_in, dec_my, dec_in,
    x0, h1, h2, go, spare, n1, q_s, kv, o_f, o_b, s_f, p_b, lse_e, sum_e, nb, u, act,
    eo, ckv, dckv, gp_s, gp_r, gown, d_o, dkv, dkv_r, gj, dl,
    y0, a1, m_b, sqkv, so, dx_s, dx_r, cq, cp, cp_b, st_p, st_r, co_r, co, co_b,
    px_s, px_r, a2, a3, du, dact, f_b, tgt, acc, acc_b, acc_r, vl_s, vl_r, gffn, gco, st_g,
    load_sem, ring_sem, send_sem, recv_sem,
):
    width = x0.shape[1]
    rows = x0.shape[0]
    half = f_b.shape[0]
    own = co.shape[1]
    pairs_e, pairs_d = width // LANES, own // LANES
    head, chip = lax.axis_index("head"), lax.axis_index("chip")
    mate, across = 1 - head, 1 - chip
    me, slot_mate = 2 * chip + head, 2 * chip + mate
    slot_across, slot_diag = 2 * across + head, 2 * across + mate
    to_mate, to_across = {"head": mate}, {"chip": across}
    to_diag = {"chip": across, "head": mate}

    barrier = pltpu.get_barrier_semaphore()
    for peer in (to_mate, to_across, to_diag):
        pl.semaphore_signal(barrier, inc=1, device_id=peer, device_id_type=MESH)

    def load(index, source, target):
        copy = pltpu.make_async_copy(source, target, load_sem.at[index])
        copy.start()
        return copy

    my_rows = pl.ds(pl.multiple_of(head * rows, rows), rows)
    mate_rows = pl.ds(pl.multiple_of(mate * rows, rows), rows)
    dec_rows = pl.ds(2 * rows, dec_my.shape[0])
    load_x = load(0, picked.at[my_rows], enc_my)
    load_y = load(1, picked.at[dec_rows], dec_my)
    load_qkv = load(2, enc_qkv, w_qkv)
    load_dqkv = load(3, dec_qkv, w_dqkv)
    load_do = load(4, dec_wo, w_do)
    load_cq = load(5, cross_q, w_cq)
    load_o = load(6, enc_wo, w_o)
    load_1 = load(7, enc_w1, w_1)
    load_2 = load(8, enc_w2, w_2)
    load_ckv = load(9, cross_kv, w_ckv)
    load_co = load(10, cross_wo, w_co)
    load_d1 = load(11, dec_w1, w_d1)
    load_d2 = load(12, dec_w2, w_d2)

    vocab = embedding.shape[0]
    full = vocab // CHUNK
    tail = vocab - full * CHUNK

    def chunk_copy(index, slot):
        at = pl.ds(pl.multiple_of(index * CHUNK, CHUNK), CHUNK)
        return pltpu.make_async_copy(embedding.at[at], ring.at[slot], ring_sem.at[slot])

    def tail_copy():
        slot = full % RING
        return pltpu.make_async_copy(
            embedding.at[pl.ds(full * CHUNK, tail)], ring.at[slot, pl.ds(0, tail)], ring_sem.at[slot]
        )

    for index in range(RING):
        chunk_copy(index, index).start()

    pl.semaphore_wait(barrier, 3)
    sends = []

    def send(index, source, target, peer):
        copy = pltpu.make_async_remote_copy(
            src_ref=source,
            dst_ref=target,
            send_sem=send_sem.at[index],
            recv_sem=recv_sem.at[index],
            device_id=peer,
            device_id_type=MESH,
        )
        copy.start()
        sends.append(copy)
        return copy

    got_x = send(0, picked.at[mate_rows], enc_in, to_mate)
    got_y = send(1, picked.at[dec_rows], dec_in, to_mate)

    lane = lax.broadcasted_iota(jnp.int32, (1, LANES), 1)
    low_lane = lane < HD
    low_b = jnp.where(low_lane, 1.0, 0.0).astype(BF)
    high_b = jnp.where(low_lane, 0.0, 1.0).astype(BF)
    sides = (low_b, high_b)
    gain = [gains[k : k + 1, :] for k in range(7)]

    load_x.wait()
    got_x.wait_recv()
    for block in range(rows // 64):
        part = pl.ds(block * 64, 64)
        value = enc_my[part].astype(F32) + enc_in[part].astype(F32)
        if block == 0:
            spot = lax.broadcasted_iota(jnp.int32, (64, width), 0)
            value = jnp.where(spot < PROMPT // QUARTERS, lead[...], value)
        x0[part] = value
        n1[me, part] = rms(value, gain[0]).astype(BF)
    got_n = send(2, n1.at[me], n1.at[me], to_across)
    got_m = send(3, n1.at[me], n1.at[me], to_mate)

    load_qkv.wait()

    def key_value(slot):
        def body(at):
            cols = pl.ds(pl.multiple_of(width + at.start, 256), 256)
            kv[slot, :, at] = dot_nn(n1[slot], w_qkv[:, cols]).astype(BF)

        tiles(2 * width // 256, 256, body)

    def query(at):
        q_s[:, at] = (dot_nn(n1[me], w_qkv[:, at]).astype(BF) * HD ** (-0.5)).astype(BF)

    key_value(me)
    tiles(width // 256, 256, query)
    got_m.wait_recv()
    key_value(slot_mate)

    load_y.wait()
    got_y.wait_recv()
    all_tgt = y0.shape[0]
    value = dec_my[0:all_tgt].astype(F32) + dec_in[0:all_tgt].astype(F32)
    y0[...] = value
    m_b[...] = rms(value, gain[3]).astype(BF)
    tgt[...] = dec_my[all_tgt : all_tgt + half].astype(F32) + dec_in[all_tgt : all_tgt + half].astype(F32)
    load_dqkv.wait()

    def self_cols(at):
        sqkv[:, at] = dot_nn(m_b[...], w_dqkv[:, at]).astype(BF)

    tiles(3 * own // 384, 384, self_cols)
    row_at = lax.broadcasted_iota(jnp.int32, (all_tgt, all_tgt), 0)
    col_at = lax.broadcasted_iota(jnp.int32, (all_tgt, all_tgt), 1)
    for pair in range(pairs_d):
        lo = pair * LANES
        q2 = sqkv[:, lo : lo + LANES]
        k2 = sqkv[:, own + lo : own + lo + LANES]
        v2 = sqkv[:, 2 * own + lo : 2 * own + lo + LANES]
        outs = []
        for side in sides:
            scores = dot_nt(q2 * side, k2) * HD ** (-0.5)
            scores = jnp.where(col_at <= row_at, scores, NEG)
            top = jnp.max(scores, axis=-1, keepdims=True)
            probs = jnp.exp(scores - top)
            total = jnp.sum(probs, axis=-1, keepdims=True)
            outs.append(dot_nn(probs.astype(BF), v2) / total)
        so[:, lo : lo + LANES] = jnp.where(low_lane, outs[0], outs[1]).astype(BF)
    load_do.wait()

    def self_out(at):
        dx_s[:, at] = dot_nn(so[...], w_do[:, at]).astype(BF)

    tiles(width // 256, 256, self_out)
    got_d = send(4, dx_s, dx_r, to_mate)

    got_n.wait_recv()
    got_f = send(5, n1.at[slot_across], n1.at[slot_across], to_mate)
    key_value(slot_across)

    got_d.wait_recv()
    value = y0[...] + (dx_s[...].astype(F32) + dx_r[...].astype(F32))
    a1[...] = value
    m_b[...] = rms(value, gain[4]).astype(BF)
    load_cq.wait()
    cq[...] = (dot_nn(m_b[...], w_cq[...]).astype(BF) * HD ** (-0.5)).astype(BF)

    got_f.wait_recv()
    key_value(slot_diag)

    keys = 4 * rows
    ok = ok_all[...] > 0.0

    def pair_lanes(at, base):
        return pl.ds(pl.multiple_of(base + at * LANES, LANES), LANES)

    def attend_pair(pair, carry):
        at = pair_lanes(pair, 0)
        q2 = q_s[:, at]
        k2 = kv[:, :, at].reshape(keys, LANES)
        v2 = kv[:, :, pair_lanes(pair, width)].reshape(keys, LANES)
        outs = []
        for index, side in enumerate(sides):
            s_f[...] = dot_nt(q2 * side, k2)
            for block in range(rows // 32):
                part = pl.ds(block * 32, 32)
                scores = jnp.where(ok, s_f[part], NEG)
                top = jnp.max(scores, axis=-1, keepdims=True)
                probs = jnp.exp(scores - top)
                total = jnp.sum(probs, axis=-1, keepdims=True)
                p_b[part] = probs.astype(BF)
                sum_e[index, part] = jnp.broadcast_to(total, (32, LANES))
                lse = jnp.broadcast_to(top + jnp.log(total), (32, LANES))
                if index == 0:
                    lse_e[pair, part] = lse
                else:
                    lse_e[pair, part] = jnp.where(low_lane, lse_e[pair, part], lse)
            outs.append(dot_nn(p_b[...], v2) / sum_e[index])
        both = jnp.where(low_lane, outs[0], outs[1])
        o_f[:, at] = both
        o_b[:, at] = both.astype(BF)
        return carry

    lax.fori_loop(0, pairs_e, attend_pair, 0)
    load_o.wait()

    def out_cols(at):
        h1[:, at] = x0[:, at] + dot_nn(o_b[...], w_o[:, at])

    tiles(width // 256, 256, out_cols)

    def norm_two(at):
        nb[at] = rms(h1[at], gain[1]).astype(BF)

    tiles(rows // 64, 64, norm_two)
    load_1.wait()

    def hidden(at):
        value = dot_nn(nb[...], w_1[:, at])
        u[:, at] = value
        act[:, at] = gelu(value).astype(BF)

    tiles(u.shape[1] // 256, 256, hidden)
    load_2.wait()

    def hidden_out(at):
        h2[:, at] = h1[:, at] + dot_nn(act[...], w_2[:, at])

    tiles(width // 256, 256, hidden_out)

    def norm_out(at):
        eo[head, at] = rms(h2[at], gain[2]).astype(BF)

    tiles(rows // 64, 64, norm_out)
    got_e = send(6, eo.at[head], eo.at[head], to_mate)
    load_ckv.wait()

    def cross_keys(slot):
        def body(at):
            ckv[slot, :, at] = dot_nn(eo[slot], w_ckv[:, at]).astype(BF)

        tiles(2 * own // 256, 256, body)

    cross_keys(head)
    got_e.wait_recv()
    cross_keys(mate)

    okc = ok_chip[...] > 0.0

    def cross_pair(pair):
        lo = pair * LANES
        k2 = ckv[:, :, lo : lo + LANES].reshape(2 * rows, LANES)
        v2 = ckv[:, :, own + lo : own + lo + LANES].reshape(2 * rows, LANES)
        return lo, cq[:, lo : lo + LANES], k2, v2

    stats = jnp.zeros((all_tgt, LANES), F32)
    for pair in range(pairs_d):
        lo, q2, k2, v2 = cross_pair(pair)
        outs = []
        for index, side in enumerate(sides):
            scores = jnp.where(okc, dot_nt(q2 * side, k2), NEG)
            top = jnp.max(scores, axis=-1, keepdims=True)
            probs = jnp.exp(scores - top)
            total = jnp.sum(probs, axis=-1, keepdims=True)
            outs.append(dot_nn(probs.astype(BF), v2) / total)
            stats = jnp.where(lane == 2 * pair + index, top + jnp.log(total), stats)
        both = jnp.where(low_lane, outs[0], outs[1])
        cp[:, lo : lo + LANES] = both
        cp_b[:, lo : lo + LANES] = both.astype(BF)
    st_p[...] = stats
    mine_t = pl.ds(pl.multiple_of(chip * half, half), half)
    theirs_t = pl.ds(pl.multiple_of(across * half, half), half)
    got_c = send(7, cp_b.at[theirs_t], co_r, to_across)
    got_s = send(8, st_p.at[theirs_t], st_r, to_across)
    got_c.wait_recv()
    got_s.wait_recv()
    l_own, l_oth = st_p[mine_t], st_r[...]
    top = jnp.maximum(l_own, l_oth)
    lse_c = top + jnp.log(jnp.exp(l_own - top) + jnp.exp(l_oth - top))
    w_own, w_oth = jnp.exp(l_own - lse_c), jnp.exp(l_oth - lse_c)

    def side_cols(array, pair):
        return jnp.where(
            low_lane, array[:, 2 * pair : 2 * pair + 1], array[:, 2 * pair + 1 : 2 * pair + 2]
        )

    for pair in range(pairs_d):
        lo = pair * LANES
        both = cp[mine_t, lo : lo + LANES] * side_cols(w_own, pair)
        both = both + co_r[:, lo : lo + LANES].astype(F32) * side_cols(w_oth, pair)
        co[:, lo : lo + LANES] = both
        co_b[:, lo : lo + LANES] = both.astype(BF)

    def exchange(index, value):
        slot = index - 9
        px_s[slot] = value.astype(BF)
        got = send(index, px_s.at[slot], px_r.at[slot], to_mate)
        got.wait_recv()
        return px_s[slot].astype(F32) + px_r[slot].astype(F32)

    load_co.wait()
    a2[...] = a1[mine_t] + exchange(9, dot_nn(co_b[...], w_co[...]))
    m_b[0:half] = rms(a2[...], gain[5]).astype(BF)
    load_d1.wait()

    def dec_hidden(at):
        value = dot_nn(m_b[0:half], w_d1[:, at])
        du[:, at] = value
        dact[:, at] = gelu(value).astype(BF)

    tiles(du.shape[1] // 512, 512, dec_hidden)
    load_d2.wait()
    a3[...] = a2[...] + exchange(10, dot_nn(dact[...], w_d2[...]))
    f_b[...] = rms(a3[...], gain[6]).astype(BF)

    acc[...] = jnp.zeros_like(acc)

    def vocab_step(logits, table, top, total):
        new_top = jnp.maximum(top, jnp.max(logits, axis=-1, keepdims=True))
        fade = jnp.exp(top - new_top)
        probs = jnp.exp(logits - new_top)
        acc[...] = acc[...] * fade + dot_nn(probs.astype(BF), table)
        return new_top, total * fade + jnp.sum(probs, axis=-1, keepdims=True)

    def vocab_chunk(index, carry):
        slot = lax.rem(index, RING)
        chunk_copy(index, slot).wait()
        table = ring[slot]
        carry = vocab_step(dot_nt(f_b[...], table), table, *carry)

        @pl.when(index + RING < full)
        def _():
            chunk_copy(index + RING, slot).start()

        @pl.when(index + RING == full)
        def _():
            tail_copy().start()

        return carry

    carry = (jnp.full((half, 1), NEG, F32), jnp.zeros((half, 1), F32))
    carry = lax.fori_loop(0, full, vocab_chunk, carry)
    tail_copy().wait()
    table = ring[full % RING, 0:tail]
    top, total = vocab_step(dot_nt(f_b[...], table), table, *carry)
    acc_b[...] = (acc[...] / total).astype(BF)
    vl_s[...] = jnp.broadcast_to(top + jnp.log(total), vl_s.shape)
    got_a = send(11, acc_b, acc_r, to_mate)
    got_v = send(12, vl_s, vl_r, to_mate)
    pick = jnp.sum(f_b[...].astype(F32) * tgt[...], axis=-1, keepdims=True)
    got_a.wait_recv()
    got_v.wait_recv()
    l_own, l_oth = vl_s[:, 0:1], vl_r[:, 0:1]
    top = jnp.maximum(l_own, l_oth)
    lse_v = top + jnp.log(jnp.exp(l_own - top) + jnp.exp(l_oth - top))
    share = weight[:, 0:1]
    loss = jnp.sum(share * (lse_v - pick), axis=0, keepdims=True) * jnp.where(head == 0, 1.0, 0.0)
    mean_row = acc_b[...].astype(F32) * jnp.exp(l_own - lse_v) + acc_r[...].astype(F32) * jnp.exp(l_oth - lse_v)
    gffn[...] = rms_grad(a3[...], gain[6], share * (mean_row - tgt[...]))

    m_b[0:half] = gffn[...].astype(BF)

    def dec_hidden_grad(at):
        value = dot_nt(m_b[0:half], w_d2[at])
        dact[:, at] = gelu_grad(du[:, at], value).astype(BF)

    tiles(du.shape[1] // 512, 512, dec_hidden_grad)
    slope = exchange(13, dot_nt(dact[...], w_d1[...]))
    gcross = gffn[...] + rms_grad(a2[...], gain[5], slope)
    gco[chip] = dot_nt(gcross.astype(BF), w_co[...]).astype(BF)
    stats = lse_c
    for pair in range(pairs_d):
        lo = pair * LANES
        value = gco[chip, :, lo : lo + LANES].astype(F32) * co[:, lo : lo + LANES]
        for index in range(2):
            picked_side = jnp.where(low_lane == (index == 0), value, 0.0)
            delta = jnp.sum(picked_side, axis=-1, keepdims=True)
            stats = jnp.where(lane == HD + 2 * pair + index, delta, stats)
    st_g[chip] = stats
    got_g = send(14, gco.at[chip], gco.at[chip], to_across)
    got_t = send(15, st_g.at[chip], st_g.at[chip], to_across)
    got_g.wait_recv()
    got_t.wait_recv()

    stats = st_g[...].reshape(all_tgt, LANES)
    for pair in range(pairs_d):
        lo, q2, k2, v2 = cross_pair(pair)
        do2 = gco[:, :, lo : lo + LANES].reshape(all_tgt, LANES)
        dks, dvs = [], []
        for index, side in enumerate(sides):
            column = 2 * pair + index
            scores = jnp.where(okc, dot_nt(q2 * side, k2), NEG)
            probs = jnp.exp(scores - stats[:, column : column + 1])
            dp = dot_nt(do2 * side, v2)
            ds = (probs * (dp - stats[:, HD + column : HD + column + 1])).astype(BF)
            dks.append(dot_tn(ds, q2))
            dvs.append(dot_tn(probs.astype(BF), do2))
        dckv[:, :, lo : lo + LANES] = jnp.where(low_lane, *dks).astype(BF).reshape(2, rows, LANES)
        dckv[:, :, own + lo : own + lo + LANES] = jnp.where(low_lane, *dvs).astype(BF).reshape(2, rows, LANES)

    def pair_grad_mate(at):
        gp_s[:, at] = dot_nt(dckv[mate], w_ckv[at]).astype(BF)

    tiles(width // 256, 256, pair_grad_mate)
    got_p = send(16, gp_s, gp_r, to_mate)

    def pair_grad_mine(at):
        gown[:, at] = dot_nt(dckv[head], w_ckv[at])

    tiles(width // 256, 256, pair_grad_mine)
    got_p.wait_recv()

    def out_grad(at):
        value = rms_grad(h2[at], gain[2], gown[at].astype(BF).astype(F32) + gp_r[at].astype(F32))
        go[at] = value
        nb[at] = value.astype(BF)

    tiles(rows // 64, 64, out_grad)

    def hidden_grad(at):
        act[:, at] = gelu_grad(u[:, at], dot_nt(nb[...], w_2[at])).astype(BF)

    tiles(u.shape[1] // 256, 256, hidden_grad)

    def norm_two_grad(at):
        spare[:, at] = dot_nt(act[...], w_1[at])

    tiles(width // 256, 256, norm_two_grad)

    def one_grad(at):
        value = go[at] + rms_grad(h1[at], gain[1], spare[at])
        go[at] = value
        nb[at] = value.astype(BF)

    tiles(rows // 64, 64, one_grad)

    def attn_grad(at):
        d_o[:, at] = dot_nt(nb[...], w_o[at]).astype(BF)

    tiles(width // 256, 256, attn_grad)

    okl = ok_lead[...] > 0.0
    lead_keys = 4 * LEAD_PAD

    def lead_pair(pair, carry):
        at = pair_lanes(pair, 0)
        vat = pair_lanes(pair, width)
        q2, do2 = q_s[:, at], d_o[:, at]
        k2 = kv[:, 0:LEAD_PAD, at].reshape(lead_keys, LANES)
        v2 = kv[:, 0:LEAD_PAD, vat].reshape(lead_keys, LANES)
        value = do2.astype(F32) * o_f[:, at]
        dks, dvs, deltas = [], [], []
        for index, side in enumerate(sides):
            delta = jnp.sum(jnp.where(low_lane == (index == 0), value, 0.0), axis=-1, keepdims=True)
            deltas.append(delta)
            lse = lse_e[pair, :, index * HD : index * HD + 1]
            scores = jnp.where(okl, dot_nt(q2 * side, k2), NEG)
            probs = jnp.exp(scores - lse)
            ds = (probs * (dot_nt(do2 * side, v2) - delta)).astype(BF)
            dks.append(dot_tn(ds, q2))
            dvs.append(dot_tn(probs.astype(BF), do2))
        dkv[:, :, at] = jnp.where(low_lane, *dks).astype(BF).reshape(4, LEAD_PAD, LANES)
        dkv[:, :, vat] = jnp.where(low_lane, *dvs).astype(BF).reshape(4, LEAD_PAD, LANES)
        dl[pair] = jnp.where(low_lane, *[d[0:LEAD_PAD] for d in deltas])
        return carry

    lax.fori_loop(0, pairs_e, lead_pair, 0)
    got_k = [
        send(17, dkv.at[slot_across], dkv_r.at[1], to_across),
        send(18, dkv.at[slot_diag], dkv_r.at[2], to_diag),
        send(19, dkv.at[slot_mate], dkv_r.at[0], to_mate),
    ]

    def query_pair(pair, carry):
        at = pair_lanes(pair, 0)
        q2, do2 = q_s[0:LEAD_PAD, at], d_o[0:LEAD_PAD, at]
        k2 = kv[:, :, at].reshape(keys, LANES)
        v2 = kv[:, :, pair_lanes(pair, width)].reshape(keys, LANES)
        dqs = []
        for index, side in enumerate(sides):
            column = slice(index * HD, index * HD + 1)
            scores = jnp.where(ok, dot_nt(q2 * side, k2), NEG)
            probs = jnp.exp(scores - lse_e[pair, 0:LEAD_PAD, column])
            ds = (probs * (dot_nt(do2 * side, v2) - dl[pair, :, column])).astype(BF)
            dqs.append(dot_nn(ds, k2) * HD ** (-0.5))
        gj[:, at] = jnp.where(low_lane, *dqs).astype(BF)
        return carry

    lax.fori_loop(0, pairs_e, query_pair, 0)
    for copy in got_k:
        copy.wait_recv()
    summed = dkv[me].astype(F32)
    for index in range(3):
        summed = summed + dkv_r[index].astype(F32)
    gj[:, width:] = summed.astype(BF)

    def start_grad(at):
        spare[0:LEAD_PAD, at] = dot_nt(gj[...], w_qkv[at])

    tiles(width // 256, 256, start_grad)
    top_rows = slice(0, LEAD_PAD)
    value = go[top_rows] + rms_grad(x0[top_rows], gain[0], spare[top_rows])
    spot = lax.broadcasted_iota(jnp.int32, (LEAD_PAD, width), 0)
    extra = jnp.where(spot == PROMPT // QUARTERS, loss, 0.0)
    out[...] = jnp.where(spot < PROMPT // QUARTERS, value, extra)
    for copy in sends:
        copy.wait_send()


def main_call(vmem, hbm):
    rows, half = 256, vmem[4].shape[0]
    wq, wo, w1, w2, dqkv, dwo, cqw, ckvw, cwo, dw1, dw2, emb = hbm[1:]
    width, own, ff, dff, tgt_all = wo.shape[0], dwo.shape[0], w1.shape[1], dw1.shape[1], 2 * half
    pairs_e = width // LANES

    def v(shape, kind=F32):
        return pltpu.VMEM(shape, kind)

    scratch = [v(w.shape, BF) for w in hbm[1:12]]
    scratch += [v((RING, CHUNK, width), BF)]
    scratch += [v((rows, width), BF), v((rows, width), BF), v((tgt_all + half, width), BF), v((tgt_all + half, width), BF)]
    scratch += [v((rows, width)) for _ in range(5)]
    scratch += [v((4, rows, width), BF), v((rows, width), BF), v((4, rows, 2 * width), BF)]
    scratch += [v((rows, width)), v((rows, width), BF), v((rows, 4 * rows)), v((rows, 4 * rows), BF)]
    scratch += [v((pairs_e, rows, LANES)), v((2, rows, LANES)), v((rows, width), BF)]
    scratch += [v((rows, ff)), v((rows, ff), BF)]
    scratch += [v((2, rows, width), BF), v((2, rows, 2 * own), BF), v((2, rows, 2 * own), BF)]
    scratch += [v((rows, width), BF), v((rows, width), BF), v((rows, width)), v((rows, width), BF)]
    scratch += [v((4, LEAD_PAD, 2 * width), BF), v((3, LEAD_PAD, 2 * width), BF), v((LEAD_PAD, 3 * width), BF)]
    scratch += [v((pairs_e, LEAD_PAD, LANES))]
    scratch += [v((tgt_all, width)), v((tgt_all, width)), v((tgt_all, width), BF), v((tgt_all, 3 * own), BF)]
    scratch += [v((tgt_all, own), BF), v((tgt_all, width), BF), v((tgt_all, width), BF), v((tgt_all, own), BF)]
    scratch += [v((tgt_all, own)), v((tgt_all, own), BF), v((tgt_all, LANES)), v((half, LANES))]
    scratch += [v((half, own), BF), v((half, own)), v((half, own), BF)]
    scratch += [v((5, half, width), BF), v((5, half, width), BF)]
    scratch += [v((half, width)), v((half, width)), v((half, dff)), v((half, dff), BF), v((half, width), BF)]
    scratch += [v((half, width)), v((half, width)), v((half, width), BF), v((half, width), BF)]
    scratch += [v((half, LANES)), v((half, LANES)), v((half, width)), v((2, half, own), BF), v((2, half, LANES))]
    scratch += [
        pltpu.SemaphoreType.DMA((13,)),
        pltpu.SemaphoreType.DMA((RING,)),
        pltpu.SemaphoreType.DMA((20,)),
        pltpu.SemaphoreType.DMA((20,)),
    ]
    any_spec, vmem_spec = pl.BlockSpec(memory_space=pl.ANY), pl.BlockSpec(memory_space=pltpu.VMEM)
    return pl.pallas_call(
        main_kernel,
        out_shape=jax.ShapeDtypeStruct((LEAD_PAD, width), F32),
        in_specs=[any_spec] + [vmem_spec] * len(vmem) + [any_spec] * len(hbm[1:]),
        out_specs=vmem_spec,
        scratch_shapes=scratch,
        compiler_params=pltpu.CompilerParams(
            collective_id=1, has_side_effects=True, vmem_limit_bytes=62 * 1024 * 1024
        ),
        name="step_of_one_example",
    )(hbm[0], *vmem, *hbm[1:])


def lamb_terms(clipped, first_old, second_old, param):
    first_next = beta_first * first_old + (1.0 - beta_first) * clipped
    second_next = beta_second * second_old + (1.0 - beta_second) * clipped * clipped
    scaled_first = first_next / (1.0 - beta_first**STEP)
    scaled_second = second_next / (1.0 - beta_second**STEP)
    update = scaled_first / (jnp.sqrt(scaled_second) + adam_eps) + decay_rate * param
    return (first_next, second_next, update)


def shards(
    enc_ids,
    lengths,
    dec_ids,
    target_ids,
    loss_mask,
    embedding,
    prompt,
    first_moment,
    second_moment,
    gains,
    enc_qkv,
    enc_wo,
    enc_w1,
    enc_w2,
    dec_qkv,
    dec_wo,
    cross_q,
    cross_kv,
    cross_wo,
    dec_w1,
    dec_w2,
):
    head_idx = lax.axis_index("head")
    chip_idx = lax.axis_index("chip")
    ex_idx = lax.axis_index("ex")
    quarter = 2 * chip_idx + head_idx
    vocab_part, width = embedding.shape
    own = dec_wo.shape[0]
    offset = head_idx * vocab_part
    enc_dev, tgt_dev = enc_ids.shape[1], dec_ids.shape[1]
    seqs = lax.axis_size(SEQ)
    total_len = enc_dev * seqs
    tgt_all = tgt_dev * seqs
    half = tgt_all // 2
    tokens = (total_len - PROMPT) // QUARTERS
    lead = PROMPT // QUARTERS
    rows = total_len // QUARTERS

    ids = jnp.concatenate([enc_ids, dec_ids, target_ids], axis=1)
    every = lax.all_gather(ids, SEQ)
    ids = lax.dynamic_index_in_dim(every, ex_idx, 1, keepdims=False)
    tok_ids = ids[:, :enc_dev].reshape(-1)[PROMPT:].reshape(QUARTERS, tokens)
    tok_ids = jnp.pad(tok_ids, ((0, 0), (lead, 0)))
    chip_ids = lax.dynamic_slice_in_dim(tok_ids, 2 * chip_idx, 2, 0).reshape(-1)
    y_ids = ids[:, enc_dev : enc_dev + tgt_dev].reshape(-1)
    t_ids = lax.dynamic_slice_in_dim(ids[:, enc_dev + tgt_dev :].reshape(-1), chip_idx * half, half)
    local = jnp.concatenate([chip_ids, y_ids, t_ids]) - offset
    inside = (local >= 0) & (local < vocab_part)
    picked = jnp.take(embedding, jnp.clip(local, 0, vocab_part - 1), axis=0)
    picked = jnp.where(inside[:, None], picked, jnp.zeros((), jnp.bfloat16))
    length = lengths[ex_idx]
    slot_q = jnp.arange(QUARTERS)[:, None]
    slot_i = jnp.arange(rows)[None, :]
    key_ok = ((slot_i < lead) | (tokens * slot_q + slot_i - lead < length)).astype(F32)
    ok_all = key_ok.reshape(1, -1)
    ok_chip = lax.dynamic_slice_in_dim(key_ok, 2 * chip_idx, 2, 0).reshape(1, -1)
    ok_lead = key_ok[:, :LEAD_PAD].reshape(1, -1)
    lead_rows = lax.dynamic_slice_in_dim(prompt, quarter * lead, lead, 0)
    lead_rows = jnp.pad(lead_rows, ((0, 64 - lead), (0, 0)))
    mask = loss_mask[ex_idx].astype(F32)
    weight = lax.dynamic_slice_in_dim(mask, chip_idx * half, half) / jnp.sum(mask)
    weight = jnp.broadcast_to(weight[:, None], (half, LANES))
    scales = jnp.concatenate([gains[:6], gains[6:] * width ** (-0.5), jnp.zeros((1, width), F32)], axis=0)
    block = main_call(
        (lead_rows, ok_all, ok_chip, ok_lead, weight, scales),
        (
            picked,
            enc_qkv,
            enc_wo,
            enc_w1,
            enc_w2,
            dec_qkv.reshape(width, 3 * own),
            dec_wo,
            cross_q,
            cross_kv.reshape(width, 2 * own),
            cross_wo,
            dec_w1,
            dec_w2,
            embedding,
        ),
    )
    canvas = jnp.zeros((PROMPT + 1, width), F32)
    canvas = lax.dynamic_update_slice_in_dim(canvas, block[:lead], quarter * lead, 0)
    canvas = canvas.at[PROMPT].set(block[lead])
    summed = lax.psum(canvas, EVERYONE)
    loss = summed[PROMPT, 0]
    grad_total = summed[:PROMPT]

    grad_norm = jnp.sqrt(jnp.sum(grad_total * grad_total))
    clip_scale = clip_bound / jnp.maximum(grad_norm, clip_bound)
    first_new, second_new, update = lamb_terms(grad_total * clip_scale, first_moment, second_moment, prompt)
    param_norm = jnp.sqrt(jnp.sum(prompt * prompt))
    update_norm = jnp.sqrt(jnp.sum(update * update))
    prompt_new = prompt - learn_rate * (param_norm / update_norm) * update
    return (
        loss,
        grad_norm,
        jnp.stack([param_norm, update_norm]),
        first_new,
        second_new,
        prompt_new,
    )


def solution(mesh):
    finer = Mesh(
        mesh.devices.reshape(mesh.shape["grp"], mesh.shape["seq"] // 2, 2, mesh.shape["head"]),
        ("grp", "ex", "chip", "head"),
    )
    placed = (
        P("grp", SEQ),
        P("grp"),
        P("grp", SEQ),
        P("grp", SEQ),
        P("grp", None),
        P("head", None),
        P(),
        P(),
        P(),
        P(),
        P(),
        P(),
        P(),
        P(),
        P(None, None, "head"),
        P("head", None),
        P(None, "head"),
        P(None, None, "head"),
        P("head", None),
        P(None, "head"),
        P("head", None),
    )
    return jax.shard_map(
        shards,
        mesh=finer,
        in_specs=placed,
        out_specs=(P(), P(), P(), P(), P(), P()),
        check_vma=False,
    )
```

profile of v0, /device:TPU:1, one launch (start us, length us, event | category | flops | bytes accessed | tf_op | source)
XLA Modules:
  0.0 325.0 jit_solution(151336717045315497)
XLA Ops:
  7.2 0.0 all-reduce.4.cloned.1.call-start
  7.2 0.8 pad_add_fusion
  8.0 20.4 %all-gather = s32[128,80]{1,0:T(8,128)S(1)} all-gather(s32[8,80]{1,0:T(8,128)S(1)} %pad_add_fusion), channel_id=2, replica_groups=mesh['grp'=4,'ex'=8,'chip'=2,'head'=2] {'ex','chip'}, dimensions={0}, use_global_device_ids=true | all-gather | bytes 43520 | tf_op jit(solution)/shard_map/all_gather | solution.py:693
  28.5 0.1 fusion.14
  28.6 0.1 reshape.216
  28.7 0.1 dynamic_slice.27
  28.7 0.1 dynamic-slice_bitcast_fusion.1
  28.8 0.1 concatenate.37
  28.9 0.1 concatenate.40
  29.0 0.1 reshape.214
  29.1 0.1 slice.49
  29.2 0.1 reshape.215
  29.2 1.2 dynamic_slice.29
  30.5 0.7 fusion.2
  31.2 0.1 fusion.6
  31.3 1.3 fusion.12
  32.6 0.6 copy.33
  33.2 0.6 reshape.218.ok_lead
  33.8 0.6 copy.32
  34.4 2.6 copy.28
  37.0 0.0 copy-start.4
  37.1 2.2 copy.29.dec_qkv
  39.3 0.0 copy-done.4
  39.3 0.0 copy-start.7
  39.3 1.3 copy.34
  40.6 0.0 copy-done.7
  40.6 0.0 copy-start
  40.6 14.7 %gather_fusion = bf16[704,768]{1,0:T(8,128)(2,1)S(1)} fusion(bf16[16064,768]{1,0:T(8,128)(2,1)} %embedding.1, s32[1024]{0:T(1024)S(1)} %pad_clamp_fusion), kind=kCustom, calls=%fused_computation | custom fusion | bytes 2165504 | tf_op jit(solution)/shard_map/jit(_take)/gather | solution.py:702
  55.3 0.7 fusion.9
  56.0 0.0 copy-done
  56.0 0.7 pad.11.lead
  56.7 0.1 pad.16.clone
  56.8 1.2 select_select_fusion.picked
  58.0 0.7 maximum_maximum_fusion.gains
  58.7 0.7 broadcast_in_dim.42.weight
  59.4 103.4 %step_of_one_example.1 = f32[32,768]{1,0:T(8,128)} custom-call(bf16[704,768]{1,0:T(8,128)(2,1)} %select_select_fusion.picked, f32[64,768]{1,0:T(8,128)} %pad.11.lead, f32[1,1024]{1,0:T(1,128)} %bitcast.41, f32[1,512]{1,0:T(1,128)} %bitcast.42, f32[1,128]{1,0:T(1,128)} %reshape.218.ok_lead, f32[64,128]{1,0:T(8,128)} %broadcast_in_dim.42.weight, ...), custom_call_target="tpu_custom_call" | custom-call | tf_op jit(solution)/shard_map/step_of_one_example/pallas_call | solution.py:631
  162.8 0.0 copy-start.5
  162.9 0.0 copy-start.6
  162.9 0.8 slice.56
  163.7 1.4 dynamic_update_slice.3
  165.2 0.1 scatter.4
  165.2 0.0 copy-start.1
  165.3 0.7 copy-done.1
  166.0 0.0 all-reduce.4.cloned.1.call-update
  166.0 142.7 %all-reduce.4.cloned.1.call-done = f32[101,768]{1,0:T(8,128)} async-done(((f32[101,768]{1,0:T(8,128)}), f32[101,768]{1,0:T(8,128)}) %all-reduce.4.cloned.1.call-update) | async-done | bytes 310288 | tf_op jit(solution)/shard_map/psum | solution.py:738
  308.7 1.7 multiply_reduce_fusion.2
  311.1 0.0 copy-done.5
  311.1 0.0 copy-done.6
  311.1 1.9 multiply_reduce_fusion.1
  313.0 0.0 copy-start.2
  313.0 0.0 copy-start.3
  314.4 0.6 pad_maximum_fusion
  315.0 0.9 multiply_subtract_fusion
  315.9 1.2 slice.65
  317.1 0.0 copy-done.2
  317.1 0.0 copy-done.3
  (13 shorter events, 0.1 us)
Async XLA Ops:
  7.2 301.5 %all-reduce.4.cloned.1.call-start = ((), (), s32[]{:S(2)}) async-start(), calls=%async_computation | async-start | bytes 638976 | tf_op jit(solution)/shard_map/psum | solution.py:738
  37.0 2.3 copy-start.4
  39.3 1.3 copy-start.7
  40.6 15.4 %copy-start = (f32[100,768]{1,0:T(8,128)S(1)}, f32[100,768]{1,0:T(8,128)}, u32[]{:S(2)}) copy-start(f32[100,768]{1,0:T(8,128)} %param.29) | copy-start | bytes 921604
  162.8 148.2 %copy-start.5 = (f32[100,768]{1,0:T(8,128)S(1)}, f32[100,768]{1,0:T(8,128)}, u32[]{:S(2)}) copy-start(f32[100,768]{1,0:T(8,128)} %param.30) | copy-start | bytes 921604
  162.9 148.2 %copy-start.6 = (f32[100,768]{1,0:T(8,128)S(1)}, f32[100,768]{1,0:T(8,128)}, u32[]{:S(2)}) copy-start(f32[100,768]{1,0:T(8,128)} %param.31) | copy-start | bytes 921604
  165.2 0.7 copy-start.1
  313.0 4.1 %copy-start.2 = (f32[100,768]{1,0:T(8,128)}, f32[100,768]{1,0:T(8,128)S(1)}, u32[]{:S(2)}) copy-start(f32[100,768]{1,0:T(8,128)S(1)} %get-tuple-element.20) | copy-start | bytes 921604
  313.0 4.1 %copy-start.3 = (f32[100,768]{1,0:T(8,128)}, f32[100,768]{1,0:T(8,128)S(1)}, u32[]{:S(2)}) copy-start(f32[100,768]{1,0:T(8,128)S(1)} %get-tuple-element.21) | copy-start | bytes 921604
Sparse Core Ops, SparseCore 0:
  166.1 142.5 all-reduce.3
where the time goes:
time: 326 us; the launch traced here: 325 us
  waiting for transfers between devices  143 us (44%)
  Pallas kernels  103 us (32%)
  local copies, waits for them, and re-layouts  30.4 us (9%)
  blocking collectives  20.4 us (6%)
  between operations  17.5 us (5%)
  other arithmetic  10.5 us (3%)
    psum x1, waiting for transfers between devices, shards(): summed = lax.psum(canvas, EVERYONE)  143 us
    pallas_call x1, Pallas kernels, main_call(): pl.pallas_call(main_kernel, out_shape=jax.ShapeDtypeStruct((LEAD_PAD, wid...  103 us
    all_gather x1, blocking collectives, shards(): every = lax.all_gather(ids, SEQ)  20.4 us
    gather x1, local copies, waits for them, and re-layouts, shards(): picked = jnp.take(embedding, jnp.clip(local, 0, vocab_part - 1), axis=0)  14.7 us
  transfers between devices with their start and end apart: 1, of which 1 were waited for; matrix products, arithmetic and copies ran while one was open for 0% of the time, Pallas kernels for 0%

commit v1 on v0

--- a/solution.py
+++ b/solution.py
@@ -1,3 +1,5 @@
+import functools
+
 import jax
 import jax.numpy as jnp
 from jax import lax
@@ -80,11 +82,11 @@
 
 
 def main_kernel(
-    picked, lead, ok_all, ok_chip, ok_lead, weight, gains,
+    lengths, picked, prompt, loss_mask, gains,
     enc_qkv, enc_wo, enc_w1, enc_w2, dec_qkv, dec_wo, cross_q, cross_kv, cross_wo, dec_w1, dec_w2, embedding,
     out,
     w_qkv, w_o, w_1, w_2, w_dqkv, w_do, w_cq, w_ckv, w_co, w_d1, w_d2, ring,
-    enc_my, enc_in, dec_my, dec_in,
+    lead, enc_my, enc_in, dec_my, dec_in,
     x0, h1, h2, go, spare, n1, q_s, kv, o_f, o_b, s_f, p_b, lse_e, sum_e, nb, u, act,
     eo, ckv, dckv, gp_s, gp_r, gown, d_o, dkv, dkv_r, gj, dl,
     y0, a1, m_b, sqkv, so, dx_s, dx_r, cq, cp, cp_b, st_p, st_r, co_r, co, co_b,
@@ -107,6 +109,8 @@
     for peer in (to_mate, to_across, to_diag):
         pl.semaphore_signal(barrier, inc=1, device_id=peer, device_id_type=MESH)
 
+    ex = lax.axis_index("ex")
+
     def load(index, source, target):
         copy = pltpu.make_async_copy(source, target, load_sem.at[index])
         copy.start()
@@ -128,6 +132,7 @@
     load_co = load(10, cross_wo, w_co)
     load_d1 = load(11, dec_w1, w_d1)
     load_d2 = load(12, dec_w2, w_d2)
+    leads = PROMPT // QUARTERS
 
     vocab = embedding.shape[0]
     full = vocab // CHUNK
@@ -171,6 +176,24 @@
     high_b = jnp.where(low_lane, 0.0, 1.0).astype(BF)
     sides = (low_b, high_b)
     gain = [gains[k : k + 1, :] for k in range(7)]
+    gain[6] = gain[6] * width ** (-0.5)
+    length = lengths[ex]
+    tokens = kv.shape[1] - leads
+
+    def allowed(slots, span, first):
+        at = lax.broadcasted_iota(jnp.int32, (1, slots * span), 1)
+        slot = at // span
+        inner = at - slot * span
+        return (inner < leads) | (tokens * (slot + first) + inner - leads < length)
+
+    ok = allowed(4, rows, 0)
+    okc = allowed(2, rows, 2 * chip)
+    okl = allowed(4, LEAD_PAD, 0)
+    mask_row = loss_mask[pl.ds(ex, 1), :].astype(F32)
+    lane_at = lax.broadcasted_iota(jnp.int32, (half, mask_row.shape[1]), 1)
+    row_of = lax.broadcasted_iota(jnp.int32, (half, mask_row.shape[1]), 0)
+    own_mask = jnp.where(lane_at == row_of + chip * half, jnp.broadcast_to(mask_row, lane_at.shape), 0.0)
+    share = jnp.sum(own_mask, axis=-1, keepdims=True) / jnp.sum(mask_row, axis=-1, keepdims=True)
 
     load_x.wait()
     got_x.wait_recv()
@@ -179,7 +202,9 @@
         value = enc_my[part].astype(F32) + enc_in[part].astype(F32)
         if block == 0:
             spot = lax.broadcasted_iota(jnp.int32, (64, width), 0)
-            value = jnp.where(spot < PROMPT // QUARTERS, lead[...], value)
+            for slot in range(QUARTERS):
+                lead[0:leads] = jnp.where(me == slot, prompt[slot * leads : (slot + 1) * leads], lead[0:leads])
+            value = jnp.where(spot < leads, lead[...], value)
         x0[part] = value
         n1[me, part] = rms(value, gain[0]).astype(BF)
     got_n = send(2, n1.at[me], n1.at[me], to_across)
@@ -254,7 +279,6 @@
     key_value(slot_diag)
 
     keys = 4 * rows
-    ok = ok_all[...] > 0.0
 
     def pair_lanes(at, base):
         return pl.ds(pl.multiple_of(base + at * LANES, LANES), LANES)
@@ -330,7 +354,6 @@
     got_e.wait_recv()
     cross_keys(mate)
 
-    okc = ok_chip[...] > 0.0
 
     def cross_pair(pair):
         lo = pair * LANES
@@ -438,7 +461,6 @@
     l_own, l_oth = vl_s[:, 0:1], vl_r[:, 0:1]
     top = jnp.maximum(l_own, l_oth)
     lse_v = top + jnp.log(jnp.exp(l_own - top) + jnp.exp(l_oth - top))
-    share = weight[:, 0:1]
     loss = jnp.sum(share * (lse_v - pick), axis=0, keepdims=True) * jnp.where(head == 0, 1.0, 0.0)
     mean_row = acc_b[...].astype(F32) * jnp.exp(l_own - lse_v) + acc_r[...].astype(F32) * jnp.exp(l_oth - lse_v)
     gffn[...] = rms_grad(a3[...], gain[6], share * (mean_row - tgt[...]))
@@ -524,7 +546,6 @@
 
     tiles(width // 256, 256, attn_grad)
 
-    okl = ok_lead[...] > 0.0
     lead_keys = 4 * LEAD_PAD
 
     def lead_pair(pair, carry):
@@ -586,14 +607,15 @@
     top_rows = slice(0, LEAD_PAD)
     value = go[top_rows] + rms_grad(x0[top_rows], gain[0], spare[top_rows])
     spot = lax.broadcasted_iota(jnp.int32, (LEAD_PAD, width), 0)
-    extra = jnp.where(spot == PROMPT // QUARTERS, loss, 0.0)
-    out[...] = jnp.where(spot < PROMPT // QUARTERS, value, extra)
+    extra = jnp.where(spot == leads, loss, 0.0)
+    out[...] = jnp.where(spot < leads, value, extra)
     for copy in sends:
         copy.wait_send()
 
 
-def main_call(vmem, hbm):
-    rows, half = 256, vmem[4].shape[0]
+def main_call(lengths, vmem, hbm):
+    half = vmem[1].shape[1] // 2
+    rows = (hbm[0].shape[0] - 3 * half) // 2
     wq, wo, w1, w2, dqkv, dwo, cqw, ckvw, cwo, dw1, dw2, emb = hbm[1:]
     width, own, ff, dff, tgt_all = wo.shape[0], dwo.shape[0], w1.shape[1], dw1.shape[1], 2 * half
     pairs_e = width // LANES
@@ -603,6 +625,7 @@
 
     scratch = [v(w.shape, BF) for w in hbm[1:12]]
     scratch += [v((RING, CHUNK, width), BF)]
+    scratch += [v((64, width))]
     scratch += [v((rows, width), BF), v((rows, width), BF), v((tgt_all + half, width), BF), v((tgt_all + half, width), BF)]
     scratch += [v((rows, width)) for _ in range(5)]
     scratch += [v((4, rows, width), BF), v((rows, width), BF), v((4, rows, 2 * width), BF)]
@@ -631,23 +654,334 @@
     return pl.pallas_call(
         main_kernel,
         out_shape=jax.ShapeDtypeStruct((LEAD_PAD, width), F32),
-        in_specs=[any_spec] + [vmem_spec] * len(vmem) + [any_spec] * len(hbm[1:]),
+        in_specs=[pl.BlockSpec(memory_space=pltpu.SMEM), any_spec] + [vmem_spec] * len(vmem) + [any_spec] * len(hbm[1:]),
         out_specs=vmem_spec,
         scratch_shapes=scratch,
         compiler_params=pltpu.CompilerParams(
             collective_id=1, has_side_effects=True, vmem_limit_bytes=62 * 1024 * 1024
         ),
         name="step_of_one_example",
-    )(hbm[0], *vmem, *hbm[1:])
-
-
-def lamb_terms(clipped, first_old, second_old, param):
-    first_next = beta_first * first_old + (1.0 - beta_first) * clipped
-    second_next = beta_second * second_old + (1.0 - beta_second) * clipped * clipped
+    )(lengths, hbm[0], *vmem, *hbm[1:])
+
+
+def ids_kernel(enc_ids, dec_ids, target_ids, out, lines, got, unused, send_sem, recv_sem):
+    ex, chip = lax.axis_index("ex"), lax.axis_index("chip")
+    chips = lax.axis_size("chip")
+    seqs = lax.axis_size(SEQ)
+    me = ex * chips + chip
+    enc_dev, tgt_dev = enc_ids.shape[1], dec_ids.shape[1]
+
+    def peer_of(step):
+        peer = lax.rem(me + step, seqs)
+        row = peer // chips
+        return row, {"ex": row, "chip": lax.rem(peer, chips)}
+
+    barrier = pltpu.get_barrier_semaphore()
+
+    def greet(step, carry):
+        pl.semaphore_signal(barrier, inc=1, device_id=peer_of(step)[1], device_id_type=MESH)
+        return carry
+
+    lax.fori_loop(1, seqs, greet, 0)
+    lines[:, 0:enc_dev] = enc_ids[...]
+    lines[:, enc_dev : enc_dev + tgt_dev] = dec_ids[...]
+    lines[:, enc_dev + tgt_dev : enc_dev + 2 * tgt_dev] = target_ids[...]
+    lines[:, enc_dev + 2 * tgt_dev :] = jnp.zeros((lines.shape[0], lines.shape[1] - enc_dev - 2 * tgt_dev), jnp.int32)
+    pl.semaphore_wait(barrier, seqs - 1)
+
+    def start(step, carry):
+        row, peer = peer_of(step)
+        pltpu.make_async_remote_copy(
+            src_ref=lines.at[pl.ds(row, 1)],
+            dst_ref=got.at[pl.ds(me, 1)],
+            send_sem=send_sem,
+            recv_sem=recv_sem,
+            device_id=peer,
+            device_id_type=MESH,
+        ).start()
+        return carry
+
+    lax.fori_loop(1, seqs, start, 0)
+    own_line = lines.at[pl.ds(ex, 1)]
+    pltpu.make_async_copy(own_line, got.at[pl.ds(me, 1)], recv_sem).start()
+    pltpu.make_async_copy(own_line, unused.at[pl.ds(0, 1)], send_sem).start()
+    pltpu.make_async_copy(got, got, recv_sem).wait()
+    pltpu.make_async_copy(got, got, send_sem).wait()
+    out[...] = got[...]
+
+
+def ids_call(enc_ids, dec_ids, target_ids):
+    seqs = lax.axis_size(SEQ)
+    lanes = -(-(enc_ids.shape[1] + 2 * dec_ids.shape[1]) // LANES) * LANES
+    return pl.pallas_call(
+        ids_kernel,
+        out_shape=jax.ShapeDtypeStruct((seqs, lanes), jnp.int32),
+        in_specs=[pl.BlockSpec(memory_space=pltpu.VMEM)] * 3,
+        out_specs=pl.BlockSpec(memory_space=pltpu.VMEM),
+        scratch_shapes=[
+            pltpu.VMEM((enc_ids.shape[0], lanes), jnp.int32),
+            pltpu.VMEM((seqs, lanes), jnp.int32),
+            pltpu.VMEM((8, lanes), jnp.int32),
+            pltpu.SemaphoreType.DMA,
+            pltpu.SemaphoreType.DMA,
+        ],
+        compiler_params=pltpu.CompilerParams(collective_id=2, has_side_effects=True),
+        name="ids_of_one_example",
+    )(enc_ids, dec_ids, target_ids)
+
+
+GROUP = 16
+
+
+def lookup_kernel(rows, tokens, lead, enc_dev, tgt_dev, ids, table, out, blocks, spots, sems):
+    chip, head = lax.axis_index("chip"), lax.axis_index("head")
+    vocab_part = table.shape[0]
+    offset = head * vocab_part
+    enc_count = 2 * rows
+    tgt_all = tgt_dev * ids.shape[0]
+    half = tgt_all // 2
+    groups = out.shape[0] // GROUP
+
+    def fetch(group, place):
+        for k in range(GROUP):
+            seq_at, lane_at = place(k)
+            local = ids[seq_at, lane_at] - offset
+            inside = (local >= 0) & (local < vocab_part)
+            safe = jnp.clip(local, 0, vocab_part - 1)
+            block = safe // GROUP
+            spots[group * GROUP + k] = jnp.where(inside, k * GROUP + safe - block * GROUP, -1)
+            pltpu.make_async_copy(
+                table.at[pl.ds(pl.multiple_of(block * GROUP, GROUP), GROUP)],
+                blocks.at[group * GROUP + k],
+                sems.at[group],
+            ).start()
+
+    def fetch_enc(group, carry):
+        def place(k):
+            item = group * GROUP + k
+            slot = item // rows
+            at = (PROMPT - lead) + tokens * (2 * chip + slot) + (item - slot * rows)
+            seq_at = at // enc_dev
+            return seq_at, at - seq_at * enc_dev
+
+        fetch(group, place)
+        return carry
+
+    def fetch_tgt(base, start, lane):
+        def body(group, carry):
+            def place(k):
+                item = (group - base) * GROUP + k + start
+                seq_at = item // tgt_dev
+                return seq_at, lane + item - seq_at * tgt_dev
+
+            fetch(group, place)
+            return carry
+
+        return body
+
+    first, second = enc_count // GROUP, (enc_count + tgt_all) // GROUP
+    lax.fori_loop(0, first, fetch_enc, 0)
+    lax.fori_loop(first, second, fetch_tgt(first, 0, enc_dev), 0)
+    lax.fori_loop(second, groups, fetch_tgt(second, chip * half, enc_dev + tgt_dev), 0)
+
+    across = lax.broadcasted_iota(jnp.int32, (GROUP, GROUP * GROUP), 1)
+    down = lax.broadcasted_iota(jnp.int32, (GROUP, GROUP * GROUP), 0)
+
+    def select(group, carry):
+        at = pl.ds(pl.multiple_of(group * GROUP, GROUP), GROUP)
+        pltpu.make_async_copy(blocks.at[at], blocks.at[at], sems.at[group]).wait()
+        want = jnp.full((GROUP, GROUP * GROUP), -1, jnp.int32)
+        for k in range(GROUP):
+            want = jnp.where(down == k, spots[group * GROUP + k], want)
+        chosen = jnp.where(across == want, 1.0, 0.0).astype(BF)
+        out[at] = dot_nn(chosen, blocks[at].reshape(GROUP * GROUP, out.shape[1])).astype(BF)
+        return carry
+
+    lax.fori_loop(0, groups, select, 0)
+
+
+def lookup_call(ids, table, rows, tokens, lead, enc_dev, tgt_dev):
+    count = 2 * rows + tgt_dev * ids.shape[0] * 3 // 2
+    width = table.shape[1]
+    return pl.pallas_call(
+        functools.partial(lookup_kernel, rows, tokens, lead, enc_dev, tgt_dev),
+        out_shape=jax.ShapeDtypeStruct((count, width), BF),
+        in_specs=[pl.BlockSpec(memory_space=pltpu.SMEM), pl.BlockSpec(memory_space=pl.ANY)],
+        out_specs=pl.BlockSpec(memory_space=pltpu.VMEM),
+        scratch_shapes=[
+            pltpu.VMEM((count, GROUP, width), BF),
+            pltpu.SMEM((count,), jnp.int32),
+            pltpu.SemaphoreType.DMA((count // GROUP,)),
+        ],
+        compiler_params=pltpu.CompilerParams(vmem_limit_bytes=32 * 1024 * 1024),
+        name="embedding_rows",
+    )(ids, table)
+
+
+def sum_kernel(share, block, out, parts, unused, total, gathered, send_sem, recv_sem, out_sem, in_sem):
+    grp, ex, chip, head = (lax.axis_index(name) for name in EVERYONE)
+    n_grp, n_ex, n_chip, n_head = (lax.axis_size(name) for name in EVERYONE)
+    lead = PROMPT // QUARTERS
+    count = lead + 1
+    team = n_grp * n_ex
+    everyone = team * n_chip * n_head
+    owners = -(-count // share)
+    mine = grp * n_ex + ex
+    quarter = chip * n_head + head
+    whole = mine * QUARTERS + quarter
+
+    def device(index):
+        member, part = index // QUARTERS, lax.rem(index, QUARTERS)
+        return {
+            "grp": member // n_ex,
+            "ex": lax.rem(member, n_ex),
+            "chip": part // n_head,
+            "head": lax.rem(part, n_head),
+        }
+
+    barrier = pltpu.get_barrier_semaphore()
+
+    def greet(step, carry):
+        peer = device(lax.rem(whole + step, everyone))
+        pl.semaphore_signal(barrier, inc=1, device_id=peer, device_id_type=MESH)
+        return carry
+
+    lax.fori_loop(1, everyone, greet, 0)
+    pl.semaphore_wait(barrier, everyone - 1)
+
+    def line(ref, at, size=share):
+        return ref.at[pl.ds(at * size, size)]
+
+    def give(step, carry):
+        owner = lax.rem(mine + step, team)
+        outside = (owner < owners) & (step > 0)
+
+        @pl.when(outside)
+        def _():
+            pltpu.make_async_remote_copy(
+                src_ref=line(block, owner),
+                dst_ref=line(parts, mine),
+                send_sem=send_sem,
+                recv_sem=recv_sem,
+                device_id={"grp": owner // n_ex, "ex": lax.rem(owner, n_ex)},
+                device_id_type=MESH,
+            ).start()
+
+        @pl.when(jnp.logical_not(outside))
+        def _():
+            pltpu.make_async_copy(line(block, 0), line(unused, owner), send_sem).start()
+
+        return carry
+
+    lax.fori_loop(0, team, give, 0)
+    owning = mine < owners
+
+    @pl.when(owning)
+    def _():
+        pltpu.make_async_copy(line(block, mine), line(parts, mine), recv_sem).start()
+        pltpu.make_async_copy(parts, parts, recv_sem).wait()
+        if share == 1:
+            total[0:1] = jnp.sum(parts[...], axis=0, keepdims=True)
+        else:
+            total[0:share] = jnp.sum(parts[...].reshape(team, share, parts.shape[1]), axis=0)
+        for k in range(share):
+            row = mine * share + k
+            place = jnp.where(row < lead, quarter * lead + row, PROMPT + quarter)
+            source = line(total, k, 1)
+
+            def spread(step, carry):
+                pltpu.make_async_remote_copy(
+                    src_ref=source,
+                    dst_ref=line(gathered, place, 1),
+                    send_sem=out_sem,
+                    recv_sem=in_sem,
+                    device_id=device(lax.rem(whole + step, everyone)),
+                    device_id_type=MESH,
+                ).start()
+                return carry
+
+            lax.fori_loop(1, everyone, spread, 0)
+            pltpu.make_async_copy(source, line(gathered, place, 1), in_sem).start()
+            pltpu.make_async_copy(source, line(unused, team * share + k, 1), out_sem).start()
+
+    def wait_rows(count, sem):
+        span = gathered.at[pl.ds(0, count)]
+        pltpu.make_async_copy(span, span, sem).wait()
+
+    wait_rows(QUARTERS * owners * share, in_sem)
+    wait_rows(team * share, send_sem)
+
+    @pl.when(owning)
+    def _():
+        wait_rows(everyone * share, out_sem)
+
+    out[...] = gathered[0 : out.shape[0]]
+
+
+def sum_call(block):
+    team = lax.axis_size(("grp", "ex"))
+    count = PROMPT // QUARTERS + 1
+    share = -(-count // team)
+    width = block.shape[1]
+    rows = PROMPT + QUARTERS
+    return pl.pallas_call(
+        functools.partial(sum_kernel, share),
+        out_shape=jax.ShapeDtypeStruct((rows, width), F32),
+        in_specs=[pl.BlockSpec(memory_space=pltpu.VMEM)],
+        out_specs=pl.BlockSpec(memory_space=pltpu.VMEM),
+        scratch_shapes=[
+            pltpu.VMEM((team * share, width), F32),
+            pltpu.VMEM((team * share + max(8, share), width), F32),
+            pltpu.VMEM((max(8, share), width), F32),
+            pltpu.VMEM((max(rows, lax.axis_size(EVERYONE) * share), width), F32),
+            pltpu.SemaphoreType.DMA,
+            pltpu.SemaphoreType.DMA,
+            pltpu.SemaphoreType.DMA,
+            pltpu.SemaphoreType.DMA,
+        ],
+        compiler_params=pltpu.CompilerParams(collective_id=3, has_side_effects=True),
+        name="sum_of_prompt_gradients",
+    )(block)
+
+
+def lamb_kernel(summed, first_old, second_old, prompt, loss, grad_norm, norms, first_new, second_new, prompt_new):
+    grad = summed[0:PROMPT]
+    loss[0] = jnp.sum(summed[PROMPT : PROMPT + QUARTERS, 0:1])
+    norm = jnp.sqrt(jnp.sum(grad * grad))
+    grad_norm[0] = norm
+    clipped = grad * (clip_bound / jnp.maximum(norm, clip_bound))
+    first_next = beta_first * first_old[...] + (1.0 - beta_first) * clipped
+    second_next = beta_second * second_old[...] + (1.0 - beta_second) * clipped * clipped
+    first_new[...] = first_next
+    second_new[...] = second_next
     scaled_first = first_next / (1.0 - beta_first**STEP)
     scaled_second = second_next / (1.0 - beta_second**STEP)
+    param = prompt[...]
     update = scaled_first / (jnp.sqrt(scaled_second) + adam_eps) + decay_rate * param
-    return (first_next, second_next, update)
+    param_norm = jnp.sqrt(jnp.sum(param * param))
+    update_norm = jnp.sqrt(jnp.sum(update * update))
+    norms[0] = param_norm
+    norms[1] = update_norm
+    prompt_new[...] = param - learn_rate * (param_norm / update_norm) * update
+
+
+def lamb_call(summed, first_old, second_old, prompt):
+    smem, vmem = pl.BlockSpec(memory_space=pltpu.SMEM), pl.BlockSpec(memory_space=pltpu.VMEM)
+    like = jax.ShapeDtypeStruct(prompt.shape, F32)
+    return pl.pallas_call(
+        lamb_kernel,
+        out_shape=(
+            jax.ShapeDtypeStruct((1,), F32),
+            jax.ShapeDtypeStruct((1,), F32),
+            jax.ShapeDtypeStruct((2,), F32),
+            like,
+            like,
+            like,
+        ),
+        in_specs=[vmem] * 4,
+        out_specs=(smem, smem, smem, vmem, vmem, vmem),
+        name="lamb",
+    )(summed, first_old, second_old, prompt)
 
 
 def shards(
@@ -673,49 +1007,18 @@
     dec_w1,
     dec_w2,
 ):
-    head_idx = lax.axis_index("head")
-    chip_idx = lax.axis_index("chip")
-    ex_idx = lax.axis_index("ex")
-    quarter = 2 * chip_idx + head_idx
-    vocab_part, width = embedding.shape
+    width = embedding.shape[1]
     own = dec_wo.shape[0]
-    offset = head_idx * vocab_part
     enc_dev, tgt_dev = enc_ids.shape[1], dec_ids.shape[1]
-    seqs = lax.axis_size(SEQ)
-    total_len = enc_dev * seqs
-    tgt_all = tgt_dev * seqs
-    half = tgt_all // 2
+    total_len = enc_dev * lax.axis_size(SEQ)
+    lead = PROMPT // QUARTERS
     tokens = (total_len - PROMPT) // QUARTERS
-    lead = PROMPT // QUARTERS
     rows = total_len // QUARTERS
-
-    ids = jnp.concatenate([enc_ids, dec_ids, target_ids], axis=1)
-    every = lax.all_gather(ids, SEQ)
-    ids = lax.dynamic_index_in_dim(every, ex_idx, 1, keepdims=False)
-    tok_ids = ids[:, :enc_dev].reshape(-1)[PROMPT:].reshape(QUARTERS, tokens)
-    tok_ids = jnp.pad(tok_ids, ((0, 0), (lead, 0)))
-    chip_ids = lax.dynamic_slice_in_dim(tok_ids, 2 * chip_idx, 2, 0).reshape(-1)
-    y_ids = ids[:, enc_dev : enc_dev + tgt_dev].reshape(-1)
-    t_ids = lax.dynamic_slice_in_dim(ids[:, enc_dev + tgt_dev :].reshape(-1), chip_idx * half, half)
-    local = jnp.concatenate([chip_ids, y_ids, t_ids]) - offset
-    inside = (local >= 0) & (local < vocab_part)
-    picked = jnp.take(embedding, jnp.clip(local, 0, vocab_part - 1), axis=0)
-    picked = jnp.where(inside[:, None], picked, jnp.zeros((), jnp.bfloat16))
-    length = lengths[ex_idx]
-    slot_q = jnp.arange(QUARTERS)[:, None]
-    slot_i = jnp.arange(rows)[None, :]
-    key_ok = ((slot_i < lead) | (tokens * slot_q + slot_i - lead < length)).astype(F32)
-    ok_all = key_ok.reshape(1, -1)
-    ok_chip = lax.dynamic_slice_in_dim(key_ok, 2 * chip_idx, 2, 0).reshape(1, -1)
-    ok_lead = key_ok[:, :LEAD_PAD].reshape(1, -1)
-    lead_rows = lax.dynamic_slice_in_dim(prompt, quarter * lead, lead, 0)
-    lead_rows = jnp.pad(lead_rows, ((0, 64 - lead), (0, 0)))
-    mask = loss_mask[ex_idx].astype(F32)
-    weight = lax.dynamic_slice_in_dim(mask, chip_idx * half, half) / jnp.sum(mask)
-    weight = jnp.broadcast_to(weight[:, None], (half, LANES))
-    scales = jnp.concatenate([gains[:6], gains[6:] * width ** (-0.5), jnp.zeros((1, width), F32)], axis=0)
+    ids = ids_call(enc_ids, dec_ids, target_ids)
+    picked = lookup_call(ids, embedding, rows, tokens, lead, enc_dev, tgt_dev)
     block = main_call(
-        (lead_rows, ok_all, ok_chip, ok_lead, weight, scales),
+        lengths,
+        (prompt, loss_mask, gains),
         (
             picked,
             enc_qkv,
@@ -732,27 +1035,9 @@
             embedding,
         ),
     )
-    canvas = jnp.zeros((PROMPT + 1, width), F32)
-    canvas = lax.dynamic_update_slice_in_dim(canvas, block[:lead], quarter * lead, 0)
-    canvas = canvas.at[PROMPT].set(block[lead])
-    summed = lax.psum(canvas, EVERYONE)
-    loss = summed[PROMPT, 0]
-    grad_total = summed[:PROMPT]
-
-    grad_norm = jnp.sqrt(jnp.sum(grad_total * grad_total))
-    clip_scale = clip_bound / jnp.maximum(grad_norm, clip_bound)
-    first_new, second_new, update = lamb_terms(grad_total * clip_scale, first_moment, second_moment, prompt)
-    param_norm = jnp.sqrt(jnp.sum(prompt * prompt))
-    update_norm = jnp.sqrt(jnp.sum(update * update))
-    prompt_new = prompt - learn_rate * (param_norm / update_norm) * update
-    return (
-        loss,
-        grad_norm,
-        jnp.stack([param_norm, update_norm]),
-        first_new,
-        second_new,
-        prompt_new,
-    )
+    summed = sum_call(block)
+    loss, grad_norm, norms, first_new, second_new, prompt_new = lamb_call(summed, first_moment, second_moment, prompt)
+    return loss.reshape(()), grad_norm.reshape(()), norms, first_new, second_new, prompt_new
 
 
 def solution(mesh):

time: 326 us -> 177 us (0.54)
  waiting for transfers between devices: 143 us -> 0 us
  Pallas kernels: 103 us -> 168 us
  local copies, waits for them, and re-layouts: 30.4 us -> 7.8 us
  blocking collectives: 20.4 us -> 0 us
  between operations: 17.5 us -> 0.86 us
  other arithmetic: 10.5 us -> 0 us
    psum x1 -> x0, waiting for transfers between devices: 143 us -> none  [shards(): summed = lax.psum(canvas, EVERYONE)]
    pallas_call x0 -> x4, Pallas kernels: none -> 62.3 us  [the longest x1 25 us: sum_call(): pl.pallas_call(functools.partial(sum_kernel, share), out_shape=jax.ShapeD...]
    all_gather x1 -> x0, blocking collectives: 20.4 us -> none  [shards(): every = lax.all_gather(ids, SEQ)]
    gather x1 -> x0, local copies, waits for them, and re-layouts: 14.7 us -> none  [shards(): picked = jnp.take(embedding, jnp.clip(local, 0, vocab_part - 1), axis=0)]
    reduce_sum x3 -> x0, other arithmetic: 4.81 us -> none  [the longest x1 1.86 us: shards(): param_norm = jnp.sqrt(jnp.sum(prompt * prompt))]
  transfers between devices with their start and end apart: 1 -> 0, of which waited for: 1 -> 0; matrix products, arithmetic and copies ran while one was open for 0% -> 0% of each run, Pallas kernels for 0% -> 0%
where the time goes in v1:
time: 177 us
  Pallas kernels  168 us (95%)
  local copies, waits for them, and re-layouts  7.8 us (4%)
    pallas_call x1, Pallas kernels, main_call(): pl.pallas_call(main_kernel, out_shape=jax.ShapeDtypeStruct((LEAD_PAD, wid...  106 us
    pallas_call x1, Pallas kernels, sum_call(): pl.pallas_call(functools.partial(sum_kernel, share), out_shape=jax.ShapeD...  25 us
    pallas_call x1, Pallas kernels, lookup_call(): pl.pallas_call(functools.partial(lookup_kernel, rows, tokens, lead, enc_d...  23 us
    pallas_call x1, Pallas kernels, ids_call(): pl.pallas_call(ids_kernel, out_shape=jax.ShapeDtypeStruct((seqs, lanes),...  11.4 us
    unnamed x8, local copies, waits for them, and re-layouts  5.55 us

profile of v1, /device:TPU:1, one launch (start us, length us, event | category | flops | bytes accessed | tf_op | source)
XLA Modules:
  0.0 176.6 jit_solution(14406993701450982852)
XLA Ops:
  0.6 2.6 %copy.28 = bf16[768,3,384]{0,2,1:T(8,128)(2,1)S(1)} copy(bf16[768,3,384]{2,0,1:T(8,128)(2,1)} %param.35) | data formatting | bytes 3538944 | tf_op args[14]
  3.3 0.0 copy-start.2
  3.3 2.3 %copy.29.dec_qkv = bf16[768,1152]{1,0:T(8,128)(2,1)} copy(bf16[768,1152]{0,1:T(8,128)(2,1)S(1)} %bitcast.5) | data formatting | bytes 3538944 | tf_op jit(solution)/shard_map/reshape | solution.py:1028
  5.5 0.0 copy-done.2
  5.5 1.2 copy.30
  6.8 11.4 %ids_of_one_example.1.ids = s32[16,128]{1,0:T(8,128)} custom-call(s32[8,64]{1,0:T(8,128)} %enc_ids.1, s32[8,8]{1,0:T(8,128)} %dec_ids.1, s32[8,8]{1,0:T(8,128)} %target_ids.1), custom_call_target="tpu_custom_call" | custom-call | tf_op jit(solution)/shard_map/ids_of_one_example/pallas_call | solution.py:716
  18.2 0.0 copy-start.1
  18.2 0.7 copy-done.1
  18.9 23.0 %embedding_rows.1.picked = bf16[704,768]{1,0:T(8,128)(2,1)S(1)} custom-call(s32[16,128]{1,0:T(8,128)S(1)} %copy-done.1, bf16[16064,768]{1,0:T(8,128)(2,1)} %embedding.1), custom_call_target="tpu_custom_call" | custom-call | tf_op jit(solution)/shard_map/embedding_rows/pallas_call | solution.py:806
  41.9 0.0 copy-start
  41.9 1.0 copy-done
  42.9 105.6 %step_of_one_example.1.block = f32[32,768]{1,0:T(8,128)} custom-call(s32[8]{0:T(128)} %lengths.1, bf16[704,768]{1,0:T(8,128)(2,1)} %copy-done, f32[100,768]{1,0:T(8,128)} %prompt.3, s32[8,128]{1,0:T(8,128)} %loss_mask.1, f32[7,768]{1,0:T(8,128)} %gains.1, bf16[768,2304]{1,0:T(8,128)(2,1)} %enc_qkv.1, bf16[768,768]{1,0:T(8,128)(2,1)} %enc_wo.1, ...), custom_call_target="tpu_custom_call" | custom-call | tf_op jit(solution)/shard_map/step_of_one_example/pallas_call | solution.py:654
  148.5 25.0 %sum_of_prompt_gradients.1.summed = f32[104,768]{1,0:T(8,128)} custom-call(f32[32,768]{1,0:T(8,128)} %step_of_one_example.1.block), custom_call_target="tpu_custom_call" | custom-call | tf_op jit(solution)/shard_map/sum_of_prompt_gradients/pallas_call | solution.py:927
  173.5 2.9 %lamb.1 = (f32[1]{0:T(128)}, f32[1]{0:T(128)}, f32[2]{0:T(128)}, f32[100,768]{1,0:T(8,128)}, f32[100,768]{1,0:T(8,128)}, /*index=5*/f32[100,768]{1,0:T(8,128)}) custom-call(f32[104,768]{1,0:T(8,128)} %sum_of_prompt_gradients.1.summed, f32[100,768]{1,0:T(8,128)} %first_old.1, f32[100,768]{1,0:T(8,128)} %second_old.1, f32[100,768]{1,0:T(8,128)} %prompt.3), custom_call_target="tpu_custom_call" | custom-call | tf_op jit(solution)/shard_map/lamb/pallas_call | solution.py:971
Async XLA Ops:
  3.3 2.3 %copy-start.2 = (bf16[768,2,384]{2,1,0:T(2,128)(2,1)S(1)}, bf16[768,2,384]{2,1,0:T(2,128)(2,1)}, u32[]{:S(2)}) copy-start(bf16[768,2,384]{2,1,0:T(2,128)(2,1)} %param.38) | copy-start | bytes 3538948
  18.2 0.7 copy-start.1
  41.9 1.0 copy-start
